TPU v7x, 32 devices: a whole 2x2x4 slice. The times are simulated.
32 devices in a mesh: mp: 2 (over core), heads: 8 (over z, y), tok: 2 (over x).
Axes of the slice: x: 2, y: 2, z: 4, core: 2. Of those that a mesh axis runs over, the one named last changes fastest.
Arguments:
- context: bfloat16 [2, 512, 8192], P('mp', None, 'heads'), may hold values from -6 to 6
- out_weight: bfloat16 [2, 8192, 8192], P('mp', 'heads', 'tok'), may hold values from -0.0625 to 0.0625
- skip_states: bfloat16 [2, 512, 8192], P(None, None, 'tok'), may hold values from -6 to 6
- gram_old: float32 [8192, 8192], P('tok', ('mp', 'heads')), may hold values from -1 to 3
- cross_old: float32 [8192, 8192], P('tok', ('mp', 'heads')), may hold values from -30 to 30
- map_old: float32 [8192, 8192], P('tok', ('mp', 'heads')), may hold values from -0.3 to 0.3
Outputs:
- gram_new: float32 [8192, 8192], P('tok', ('mp', 'heads'))
- cross_new: float32 [8192, 8192], P('tok', ('mp', 'heads'))
- map_new: float32 [8192, 8192], P('tok', ('mp', 'heads'))
- residual_new: float32 [8192, 8192], P('tok', ('mp', 'heads'))
All inputs are finite; a program needn't handle non-finite values.
Results may differ from a plain program's by a relative error of at most 0.03.
Values may be sent and summed in bfloat16 or wider, within the bound.
A program may use at most 256 MiB of HBM per device.

v0:
```python
import jax
import jax.numpy as jnp
from jax import lax
from jax.sharding import PartitionSpec as P

decay_keep = 0.75
ridge_weight = 0.1
f32, bf16 = (jnp.float32, jnp.bfloat16)
CHUNKS = 4


def dot(a, b):
    return jnp.dot(a, b, preferred_element_type=f32)


def token_inner(left, right):
    return lax.dot_general(left, right, (((0,), (0,)), ((), ())), preferred_element_type=f32)


def shifted(block, axis, shift):
    n = lax.axis_size(axis)
    return lax.ppermute(block, axis, [(i, (i + shift) % n) for i in range(n)])


def total_over(value, axis):
    n = lax.axis_size(axis)
    if n & n - 1:
        return lax.psum(value, axis)
    bit = 1
    while bit < n:
        value = value + lax.ppermute(value, axis, [(i, i ^ bit) for i in range(n)])
        bit *= 2
    return value


def sum_tok(value):
    n = lax.axis_size("tok")
    half = value.astype(bf16)
    for shift in range(1, n):
        value = value + shifted(half, "tok", shift).astype(f32)
    return value.astype(bf16)


def make_states(context, out_weight, skip_states, width):
    n_tok, n_heads, n_mp = (lax.axis_size(a) for a in ("tok", "heads", "mp"))
    t, h, k = (lax.axis_index(a) for a in ("tok", "heads", "mp"))
    tokens, features = skip_states.shape[1:]
    share = features // n_heads
    part = dot(context[0], out_weight[0]).astype(bf16)
    mine = lax.psum_scatter(part, "heads", scatter_dimension=1, tiled=True)
    skip = lax.dynamic_slice(skip_states, (k, 0, h * share), (1, tokens, share))[0]
    mine = (mine.astype(f32) + skip.astype(f32)).astype(bf16)
    other = lax.ppermute(mine, "mp", [(0, 1), (1, 0)])
    pair = jnp.stack([jnp.where(k == 0, mine, other), jnp.where(k == 0, other, mine)])
    if share == width and n_tok == n_mp == 2:
        away = lax.ppermute(pair, ("mp", "tok"), [(0, 1), (3, 2)])
        columns = jnp.where(k == t, pair, away)
        half = lax.dynamic_slice_in_dim(pair[0], k * (tokens // 2), tokens // 2, 0)
        rows = lax.all_gather(half, "heads", axis=1, tiled=True)
        rows_other = lax.ppermute(rows, "mp", [(0, 1), (1, 0)])
        first = jnp.where(k == 0, rows, rows_other)
        second = jnp.where(k == 0, rows_other, rows)
        source = jnp.concatenate([first, second], 0)
        return (source, columns[0], columns[1])
    both = lax.all_gather(pair, "heads", axis=2, tiled=True)
    whole = lax.all_gather(both, "tok", axis=2, tiled=True)
    columns = lax.dynamic_slice_in_dim(whole, (k * n_heads + h) * width, width, 2)
    return (both[0], columns[0], columns[1])


def per_device(context, out_weight, skip_states, gram_old, cross_old, map_old):
    n_tok = lax.axis_size("tok")
    t = lax.axis_index("tok")
    tokens = context.shape[1]
    height, width = gram_old.shape
    new_weight = (1.0 - decay_keep) / tokens
    step = height // CHUNKS
    cuts = [slice(c * step, (c + 1) * step) for c in range(CHUNKS)]
    map_half = map_old.astype(bf16)
    gram_old_half = gram_old.astype(bf16)
    panels = [
        lax.all_gather(gram_old_half[cut], ("mp", "heads"), axis=1, tiled=True) for cut in cuts
    ]
    maps = [map_half] + [shifted(map_half, "tok", s) for s in range(1, n_tok)]
    source, source_cols, target_cols = make_states(context, out_weight, skip_states, width)
    gram_new = decay_keep * gram_old + new_weight * token_inner(source, source_cols)
    cross_new = decay_keep * cross_old + new_weight * token_inner(source, target_cols)

    def panel_part(panel, s):
        owner = lax.rem(t - s + n_tok, n_tok)
        return lax.dynamic_slice_in_dim(panel, owner * height, height, 1)

    inner_map = sum_tok(dot(source, map_half))
    residuals, halves = ([], [])
    for cut, panel in zip(cuts, panels):
        product = sum((dot(panel_part(panel, s), maps[s]) for s in range(n_tok)))
        low_rank = token_inner(source[:, cut], inner_map)
        residual = (
            cross_new[cut]
            - decay_keep * product
            - new_weight * low_rank
            - ridge_weight * map_old[cut]
        )
        residuals.append(residual)
        halves.append(residual.astype(bf16))
    away = [[shifted(half, "tok", s) for half in halves] for s in range(1, n_tok)]
    inner_residual = sum_tok(sum((dot(source[:, cut], half) for cut, half in zip(cuts, halves))))
    blocks = [jnp.concatenate(halves, 0)] + [jnp.concatenate(a, 0) for a in away]
    applied, squares, mixed = ([], 0.0, 0.0)
    for cut, panel, residual in zip(cuts, panels, residuals):
        product = sum((dot(panel_part(panel, s), blocks[s]) for s in range(n_tok)))
        low_rank = token_inner(source[:, cut], inner_residual)
        value = decay_keep * product + new_weight * low_rank + ridge_weight * residual
        applied.append(value)
        squares = squares + jnp.sum(residual * residual)
        mixed = mixed + jnp.sum(residual * value)
    totals = jnp.stack([squares, mixed])
    for axis in ("mp", "tok", "heads"):
        totals = total_over(totals, axis)
    step_size = totals[0] / totals[1]
    residual = jnp.concatenate(residuals, 0)
    return (
        gram_new,
        cross_new,
        map_old + step_size * residual,
        residual - step_size * jnp.concatenate(applied, 0),
    )


def solution(mesh):
    block = P("tok", ("mp", "heads"))
    placed = (
        P("mp", None, "heads"),
        P("mp", "heads", "tok"),
        P(None, None, "tok"),
        block,
        block,
        block,
    )
    return jax.shard_map(
        per_device, mesh=mesh, in_specs=placed, out_specs=(block,) * 4, check_vma=False
    )
```

profile of v0, /device:TPU:0, one launch (start us, length us, event | category | flops | bytes accessed | tf_op | source)
XLA Modules:
  0.0 842.1 jit_solution(6807376808990272788)
XLA Ops:
  8.4 9.4 %fusion.35 = bf16[512,4096]{1,0:T(8,128)(2,1)} fusion(bf16[1,1024,4096]{2,1,0:T(8,128)(2,1)} %param.7, bf16[1,512,1024]{2,1,0:T(8,128)(2,1)S(1)} %copy-done), kind=kOutput, calls=%fused_computation.49 | convolution fusion | flops 4297064448 | bytes 13631488 | tf_op jit(solution)/shard_map/dot_general | solution.py:13
  17.9 91.3 %reduce-scatter.2.cloned.1.call-done = bf16[512,512]{1,0:T(8,128)(2,1)} async-done(((bf16[512,4096]{1,0:T(8,128)(2,1)}), bf16[512,512]{1,0:T(8,128)(2,1)}) %reduce-scatter.2.cloned.1.call-update) | async-done | bytes 524304 | tf_op jit(solution)/shard_map/reduce_scatter | solution.py:50
  109.1 1.3 fusion.53
  110.6 1.9 collective-permute-done
  113.3 3.9 convert_element_type.56
  117.3 2.1 fusion.77
  121.1 43.2 %all-gather.6.cloned.1.call-done = bf16[256,4096]{1,0:T(8,128)(2,1)} async-done(((bf16[256,512]{1,0:T(8,128)(2,1)}), bf16[256,4096]{1,0:T(8,128)(2,1)}) %all-gather.6.cloned.1.call-update) | async-done | bytes 2097168 | tf_op jit(solution)/shard_map/all_gather | solution.py:59
  164.4 3.4 collective-permute-start.2
  167.8 6.0 convert_element_type.57
  173.8 11.4 %collective-permute-done.2 = bf16[2,512,512]{2,1,0:T(8,128)(2,1)S(1)} collective-permute-done((bf16[2,512,512]{2,1,0:T(8,128)(2,1)S(1)}, bf16[2,512,512]{2,1,0:T(8,128)(2,1)S(1)}, u32[]{:S(2)}, u32[]{:S(2)}) %collective-permute-start.2) | collective-permute-done | bytes 1048608 | tf_op jit(solution)/shard_map/ppermute | solution.py:56
  185.3 2.6 broadcast_select_fusion.1
  188.0 5.4 fusion.79
  193.4 2.6 collective-permute-start.4
  196.0 5.0 multiply_add_fusion.2
  201.0 4.9 multiply_add_fusion.1
  205.9 1.8 fusion.50
  207.7 73.5 %collective-permute-done.4 = bf16[512,512]{1,0:T(8,128)(2,1)S(1)} collective-permute-done((bf16[512,512]{1,0:T(8,128)(2,1)S(1)}, bf16[512,512]{1,0:T(8,128)(2,1)S(1)}, u32[]{:S(2)}, u32[]{:S(2)}) %collective-permute-start.4) | collective-permute-done | bytes 524320 | tf_op jit(solution)/shard_map/ppermute | solution.py:22
  281.4 14.3 %all-gather.10.cloned.1.call-done = bf16[1024,8192]{1,0:T(8,128)(2,1)} async-done(((bf16[1024,512]{1,0:T(8,128)(2,1)}), bf16[1024,8192]{1,0:T(8,128)(2,1)}) %all-gather.10.cloned.1.call-update) | async-done | bytes 16777232 | tf_op jit(solution)/shard_map/all_gather | solution.py:82
  295.7 8.3 fusion.25
  304.0 1.9 copy-done.24
  305.9 6.6 fusion.21
  312.5 5.0 fusion.82
  317.5 1.4 collective-permute-start.6
  318.9 107.4 %all-gather.12.cloned.1.call-done = bf16[1024,8192]{1,0:T(8,128)(2,1)} async-done(((bf16[1024,512]{1,0:T(8,128)(2,1)}), bf16[1024,8192]{1,0:T(8,128)(2,1)}) %all-gather.12.cloned.1.call-update) | async-done | bytes 16777232 | tf_op jit(solution)/shard_map/all_gather | solution.py:82
  426.4 8.3 fusion.13
  434.7 1.9 copy-done.23
  436.6 6.7 fusion.17
  443.3 5.0 fusion.81
  448.3 1.4 collective-permute-start.7
  449.7 107.4 %all-gather.14.cloned.1.call-done = bf16[1024,8192]{1,0:T(8,128)(2,1)} async-done(((bf16[1024,512]{1,0:T(8,128)(2,1)}), bf16[1024,8192]{1,0:T(8,128)(2,1)}) %all-gather.14.cloned.1.call-update) | async-done | bytes 16777232 | tf_op jit(solution)/shard_map/all_gather | solution.py:82
  557.1 8.5 %fusion.5 = f32[1024,512]{1,0:T(8,128)S(1)} fusion(bf16[4096,512]{1,0:T(8,128)(2,1)} %collective-permute-done.3, bf16[1024,8192]{1,0:T(8,128)(2,1)} %all-gather.14.cloned.1.call-done, s32[]{:T(128)S(6)} %select_n.73), kind=kOutput, calls=%fused_computation.10 | convolution fusion | flops 4294967296 | bytes 14680068 | tf_op jit(solution)/shard_map/dot_general | solution.py:13
  565.5 1.7 copy-done.22
  567.2 6.7 fusion.9
  574.0 5.3 fusion.80
  579.3 1.4 collective-permute-start.8
  580.7 2.9 fusion.85
  583.6 2.9 fusion.86
  586.6 2.9 fusion.87
  589.5 98.3 %all-gather.8.cloned.1.call-done = bf16[1024,8192]{1,0:T(8,128)(2,1)} async-done(((bf16[1024,512]{1,0:T(8,128)(2,1)}), bf16[1024,8192]{1,0:T(8,128)(2,1)}) %all-gather.8.cloned.1.call-update) | async-done | bytes 16777232 | tf_op jit(solution)/shard_map/all_gather | solution.py:82
  687.8 8.3 fusion.29
  697.2 6.6 fusion.33
  703.9 3.6 fusion.83
  707.4 1.5 collective-permute-start.5
  710.3 9.2 %fusion.31 = f32[1024,512]{1,0:T(8,128)S(1)} fusion(bf16[1024,8192]{1,0:T(8,128)(2,1)} %all-gather.8.cloned.1.call-done, s32[]{:T(128)S(6)} %select_n.72, bf16[1024,512]{1,0:T(8,128)(2,1)} %get-tuple-element.29, bf16[1024,512]{1,0:T(8,128)(2,1)} %get-tuple-element.31, bf16[1024,512]{1,0:T(8,128)(2,1)} %get-tuple-element.33, ...), kind=kOutput, calls=%fused_computation.36 | convolution fusion | flops 4311744512 | bytes 14680068 | tf_op jit(solution)/shard_map/dot_general | solution.py:13
  719.6 8.8 %fusion.23 = f32[1024,512]{1,0:T(8,128)S(1)} fusion(bf16[1024,8192]{1,0:T(8,128)(2,1)} %all-gather.10.cloned.1.call-done, s32[]{:T(128)S(6)} %select_n.72, bf16[1024,512]{1,0:T(8,128)(2,1)} %get-tuple-element.29, bf16[1024,512]{1,0:T(8,128)(2,1)} %get-tuple-element.31, bf16[1024,512]{1,0:T(8,128)(2,1)} %get-tuple-element.33, ...), kind=kOutput, calls=%fused_computation.28 | convolution fusion | flops 4311744512 | bytes 14680068 | tf_op jit(solution)/shard_map/dot_general | solution.py:13
  728.4 10.0 %fusion.15 = f32[1024,512]{1,0:T(8,128)} fusion(bf16[1024,8192]{1,0:T(8,128)(2,1)} %all-gather.12.cloned.1.call-done, s32[]{:T(128)S(6)} %select_n.72, bf16[1024,512]{1,0:T(8,128)(2,1)} %get-tuple-element.29, bf16[1024,512]{1,0:T(8,128)(2,1)} %get-tuple-element.31, bf16[1024,512]{1,0:T(8,128)(2,1)} %get-tuple-element.33, ...), kind=kOutput, calls=%fused_computation.20 | convolution fusion | flops 4311744512 | bytes 14680068 | tf_op jit(solution)/shard_map/dot_general | solution.py:13
  738.4 10.1 %fusion.7 = f32[1024,512]{1,0:T(8,128)} fusion(bf16[1024,8192]{1,0:T(8,128)(2,1)} %all-gather.14.cloned.1.call-done, s32[]{:T(128)S(6)} %select_n.72, bf16[1024,512]{1,0:T(8,128)(2,1)} %get-tuple-element.29, bf16[1024,512]{1,0:T(8,128)(2,1)} %get-tuple-element.31, bf16[1024,512]{1,0:T(8,128)(2,1)} %get-tuple-element.33, ...), kind=kOutput, calls=%fused_computation.12 | convolution fusion | flops 4311744512 | bytes 14680068 | tf_op jit(solution)/shard_map/dot_general | solution.py:13
  748.8 1.3 constant_dynamic-update-slice_fusion.2
  752.7 8.6 %fusion.27 = f32[1024,512]{1,0:T(8,128)S(1)} fusion(bf16[4096,512]{1,0:T(8,128)(2,1)S(1)} %constant_dynamic-update-slice_fusion, bf16[1024,8192]{1,0:T(8,128)(2,1)} %all-gather.8.cloned.1.call-done, s32[]{:T(128)S(6)} %select_n.73), kind=kOutput, calls=%fused_computation.32 | convolution fusion | flops 4294967296 | bytes 14680068 | tf_op jit(solution)/shard_map/dot_general | solution.py:13
  761.4 3.0 multiply_reduce_fusion.7
  764.4 7.1 fusion.19
  771.5 3.2 multiply_reduce_fusion.6
  776.0 8.3 fusion.11
  784.3 3.0 multiply_reduce_fusion.5
  788.0 8.3 fusion.3
  796.3 3.1 multiply_reduce_fusion.4
  803.9 1.5 collective-permute-start.11
  805.3 2.1 collective-permute-done.11
  807.5 1.4 collective-permute-start.12
  808.9 2.1 collective-permute-done.12
  811.0 3.5 collective-permute-done.13
  814.6 1.5 collective-permute-start.14
  816.1 2.9 collective-permute-done.14
  820.9 14.1 %fusion = (f32[4096,512]{1,0:T(8,128)}, f32[4096,512]{1,0:T(8,128)}) fusion(f32[1024,512]{1,0:T(8,128)} %get-tuple-element.42, f32[1024,512]{1,0:T(8,128)} %get-tuple-element.41, f32[1024,512]{1,0:T(8,128)} %get-tuple-element.40, f32[1024,512]{1,0:T(8,128)} %get-tuple-element.39, f32[1024,512]{1,0:T(8,128)} %get-tuple-element.30, ...), kind=kLoop, calls=%fused_computation.2 | loop fusion | flops 20971520 | bytes 41943044 | tf_op jit(solution)/shard_map/sub | solution.py:126
  (102 shorter events, 11.8 us)
Async XLA Ops:
  7.2 1.2 copy-start
  7.2 102.0 %reduce-scatter.2.cloned.1.call-start = ((), (), s32[]{:S(2)}) async-start(), calls=%async_computation.1 | async-start | bytes 4718592 | tf_op jit(solution)/shard_map/reduce_scatter | solution.py:50
  17.8 146.5 %all-gather.6.cloned.1.call-start = ((), (), s32[]{:S(2)}) async-start(), calls=%async_computation.2 | async-start | bytes 2359296 | tf_op jit(solution)/shard_map/all_gather | solution.py:59
  110.5 2.0 collective-permute-start
  113.3 182.4 %all-gather.10.cloned.1.call-start = ((), (), s32[]{:S(2)}) async-start(), calls=%async_computation.4 | async-start | bytes 17825792 | tf_op jit(solution)/shard_map/all_gather | solution.py:82
  119.4 307.0 %all-gather.12.cloned.1.call-start = ((), (), s32[]{:S(2)}) async-start(), calls=%async_computation.5 | async-start | bytes 17825792 | tf_op jit(solution)/shard_map/all_gather | solution.py:82
  119.9 437.1 %all-gather.14.cloned.1.call-start = ((), (), s32[]{:S(2)}) async-start(), calls=%async_computation.6 | async-start | bytes 17825792 | tf_op jit(solution)/shard_map/all_gather | solution.py:82
  120.5 567.2 %all-gather.8.cloned.1.call-start = ((), (), s32[]{:S(2)}) async-start(), calls=%async_computation.3 | async-start | bytes 17825792 | tf_op jit(solution)/shard_map/all_gather | solution.py:82
  164.3 21.0 %collective-permute-start.1 = (bf16[256,4096]{1,0:T(8,128)(2,1)}, bf16[256,4096]{1,0:T(8,128)(2,1)}, u32[]{:S(2)}, u32[]{:S(2)}) collective-permute-start(bf16[256,4096]{1,0:T(8,128)(2,1)} %all-gather.6.cloned.1.call-done), channel_id=1, source_target_pairs={{0,16},{16,0},{1,17},{17,1},{2,18},{18,2},{3,19},{19,3},{4,20},{20... | collective-permute-start | bytes 6291464 | tf_op jit(solution)/shard_map/ppermute | solution.py:60
  164.4 20.8 %collective-permute-start.2 = (bf16[2,512,512]{2,1,0:T(8,128)(2,1)S(1)}, bf16[2,512,512]{2,1,0:T(8,128)(2,1)S(1)}, u32[]{:S(2)}, u32[]{:S(2)}) collective-permute-start(bf16[2,512,512]{2,1,0:T(8,128)(2,1)S(1)} %pad_maximum_fusion.6), channel_id=1, source_target_pairs={{0,1},{17,16},{2,3},{19,18},{4,5},{21,20},{6,7},{23,22},{8,9},{25,... | collective-permute-start | bytes 3145736 | tf_op jit(solution)/shard_map/ppermute | solution.py:56
  173.8 130.2 %collective-permute-start.3 = (bf16[4096,512]{1,0:T(8,128)(2,1)}, bf16[4096,512]{1,0:T(8,128)(2,1)}, u32[]{:S(2)}, u32[]{:S(2)}) collective-permute-start(bf16[4096,512]{1,0:T(8,128)(2,1)} %convert_element_type.57), channel_id=1, source_target_pairs={{0,1},{1,0},{2,3},{3,2},{4,5},{5,4},{6,7},{7,6},{8,9},{9,8},{10,11... | collective-permute-start | bytes 12582920 | tf_op jit(solution)/shard_map/ppermute | solution.py:22
  185.3 10.7 %slice-start = ((s8[8388608]{0:T(1024)(128)(4,1)}), s8[4194304]{0:T(1024)(128)(4,1)S(1)}, s32[]{:S(2)}) async-start(s8[8388608]{0:T(1024)(128)(4,1)} %bitcast.57), calls=%async_computation.7 | async-start | bytes 8388608
  188.0 17.9 %copy-start.2 = (bf16[256,4096]{1,0:T(8,128)(2,1)}, bf16[256,4096]{1,0:T(8,128)(2,1)S(1)}, u32[]{:S(2)}) copy-start(bf16[256,4096]{1,0:T(8,128)(2,1)S(1)} %get-tuple-element.22) | copy-start | bytes 6291460
  188.0 8.0 slice-start.1
  193.4 7.6 slice-start.2
  193.4 7.6 slice-start.3
  193.4 87.8 %collective-permute-start.4 = (bf16[512,512]{1,0:T(8,128)(2,1)S(1)}, bf16[512,512]{1,0:T(8,128)(2,1)S(1)}, u32[]{:S(2)}, u32[]{:S(2)}) collective-permute-start(bf16[512,512]{1,0:T(8,128)(2,1)S(1)} %get-tuple-element.27), channel_id=1, source_target_pairs={{0,1},{1,0},{2,3},{3,2},{4,5},{5,4},{6,7},{7,6},{8,9},{9,8},{10,11... | collective-permute-start | bytes 1572872 | tf_op jit(solution)/shard_map/ppermute | solution.py:22
  295.7 10.2 %copy-start.24 = (bf16[1024,8192]{1,0:T(8,128)(2,1)S(1)}, bf16[1024,8192]{1,0:T(8,128)(2,1)}, u32[]{:S(2)}) copy-start(bf16[1024,8192]{1,0:T(8,128)(2,1)} %all-gather.10.cloned.1.call-done) | copy-start | bytes 50331652
  304.0 8.5 %copy-start.13 = (bf16[512,1024]{1,0:T(8,128)(2,1)S(1)}, bf16[512,1024]{1,0:T(8,128)(2,1)}, u32[]{:S(2)}) copy-start(bf16[512,1024]{1,0:T(8,128)(2,1)} %get-tuple-element.18) | copy-start | bytes 3145732
  317.5 431.3 %collective-permute-start.6 = (bf16[1024,512]{1,0:T(8,128)(2,1)}, bf16[1024,512]{1,0:T(8,128)(2,1)}, u32[]{:S(2)}, u32[]{:S(2)}) collective-permute-start(bf16[1024,512]{1,0:T(8,128)(2,1)} %get-tuple-element.33), channel_id=1, source_target_pairs={{0,1},{1,0},{2,3},{3,2},{4,5},{5,4},{6,7},{7,6},{8,9},{9,8},{10,11... | collective-permute-start | bytes 3145736 | tf_op jit(solution)/shard_map/ppermute | solution.py:22
  426.4 10.2 %copy-start.23 = (bf16[1024,8192]{1,0:T(8,128)(2,1)S(1)}, bf16[1024,8192]{1,0:T(8,128)(2,1)}, u32[]{:S(2)}) copy-start(bf16[1024,8192]{1,0:T(8,128)(2,1)} %all-gather.12.cloned.1.call-done) | copy-start | bytes 50331652
  436.6 6.7 copy-start.10
  448.3 301.8 %collective-permute-start.7 = (bf16[1024,512]{1,0:T(8,128)(2,1)}, bf16[1024,512]{1,0:T(8,128)(2,1)}, u32[]{:S(2)}, u32[]{:S(2)}) collective-permute-start(bf16[1024,512]{1,0:T(8,128)(2,1)} %get-tuple-element.31), channel_id=1, source_target_pairs={{0,1},{1,0},{2,3},{3,2},{4,5},{5,4},{6,7},{7,6},{8,9},{9,8},{10,11... | collective-permute-start | bytes 3145736 | tf_op jit(solution)/shard_map/ppermute | solution.py:22
  557.1 10.2 %copy-start.22 = (bf16[1024,8192]{1,0:T(8,128)(2,1)S(1)}, bf16[1024,8192]{1,0:T(8,128)(2,1)}, u32[]{:S(2)}) copy-start(bf16[1024,8192]{1,0:T(8,128)(2,1)} %all-gather.14.cloned.1.call-done) | copy-start | bytes 50331652
  567.2 6.7 copy-start.8
  574.0 6.7 copy-start.14
  574.0 9.7 %copy-start.11 = (bf16[512,1024]{1,0:T(8,128)(2,1)S(1)}, bf16[512,1024]{1,0:T(8,128)(2,1)}, u32[]{:S(2)}) copy-start(bf16[512,1024]{1,0:T(8,128)(2,1)} %get-tuple-element.19) | copy-start | bytes 3145732
  579.3 172.2 %collective-permute-start.8 = (bf16[1024,512]{1,0:T(8,128)(2,1)}, bf16[1024,512]{1,0:T(8,128)(2,1)}, u32[]{:S(2)}, u32[]{:S(2)}) collective-permute-start(bf16[1024,512]{1,0:T(8,128)(2,1)} %get-tuple-element.29), channel_id=1, source_target_pairs={{0,1},{1,0},{2,3},{3,2},{4,5},{5,4},{6,7},{7,6},{8,9},{9,8},{10,11... | collective-permute-start | bytes 3145736 | tf_op jit(solution)/shard_map/ppermute | solution.py:22
  687.8 9.4 %copy-start.25 = (bf16[1024,8192]{1,0:T(8,128)(2,1)S(1)}, bf16[1024,8192]{1,0:T(8,128)(2,1)}, u32[]{:S(2)}) copy-start(bf16[1024,8192]{1,0:T(8,128)(2,1)} %all-gather.8.cloned.1.call-done) | copy-start | bytes 50331652
  697.2 6.7 copy-start.3
  703.8 5.1 copy-start.18
  703.8 5.1 copy-start.19
  703.9 5.1 copy-start.20
  707.4 53.9 %copy-start.7 = (f32[1024,512]{1,0:T(8,128)}, f32[1024,512]{1,0:T(8,128)S(1)}, u32[]{:S(2)}) copy-start(f32[1024,512]{1,0:T(8,128)S(1)} %get-tuple-element.36) | copy-start | bytes 6291460
  707.4 41.3 %collective-permute-start.5 = (bf16[1024,512]{1,0:T(8,128)(2,1)S(1)}, bf16[1024,512]{1,0:T(8,128)(2,1)S(1)}, u32[]{:S(2)}, u32[]{:S(2)}) collective-permute-start(bf16[1024,512]{1,0:T(8,128)(2,1)S(1)} %get-tuple-element.35), channel_id=1, source_target_pairs={{0,1},{1,0},{2,3},{3,2},{4,5},{5,4},{6,7},{7,6},{8,9},{9,8},{10,11... | collective-permute-start | bytes 3145736 | tf_op jit(solution)/shard_map/ppermute | solution.py:22
  709.7 38.8 %collective-permute-start.9 = (bf16[512,512]{1,0:T(8,128)(2,1)S(1)}, bf16[512,512]{1,0:T(8,128)(2,1)S(1)}, u32[]{:S(2)}, u32[]{:S(2)}) collective-permute-start(bf16[512,512]{1,0:T(8,128)(2,1)S(1)} %get-tuple-element.37), channel_id=1, source_target_pairs={{0,1},{1,0},{2,3},{3,2},{4,5},{5,4},{6,7},{7,6},{8,9},{9,8},{10,11... | collective-permute-start | bytes 1572872 | tf_op jit(solution)/shard_map/ppermute | solution.py:22
  752.7 11.7 %copy-start.21 = (bf16[4096,512]{1,0:T(8,128)(2,1)}, bf16[4096,512]{1,0:T(8,128)(2,1)S(1)}, u32[]{:S(2)}) copy-start(bf16[4096,512]{1,0:T(8,128)(2,1)S(1)} %constant_dynamic-update-slice_fusion) | copy-start | bytes 12582916
  764.4 7.1 copy-start.4
  764.4 7.1 copy-start.15
  775.9 8.3 copy-start.5
  775.9 8.3 copy-start.12
  776.0 8.3 copy-start.17
  788.0 8.3 copy-start.6
  788.0 8.3 copy-start.9
  788.0 8.3 copy-start.16
  802.6 1.1 collective-permute-start.10
  803.9 3.5 collective-permute-start.11
  807.5 3.5 collective-permute-start.12
  811.0 3.5 collective-permute-start.13
  814.6 4.4 collective-permute-start.14
  820.9 14.1 %copy-start.1 = (bf16[1,512,1024]{2,1,0:T(8,128)(2,1)S(1)}, bf16[1,512,1024]{2,1,0:T(8,128)(2,1)}, u32[]{:S(2)}) copy-start(bf16[1,512,1024]{2,1,0:T(8,128)(2,1)} %param.6) | copy-start | bytes 3145732
Sparse Core Ops, SparseCore 0:
  17.9 91.1 reduce-scatter.1
  113.4 50.8 all-gather.5
  167.1 128.5 all-gather.9
  297.8 128.5 all-gather.11
  428.5 128.5 all-gather.13
  559.2 128.5 all-gather.7
where the time goes:
time: 848 us; the launch traced here: 842 us
  waiting for transfers between devices  562 us (66%)
  matrix products  196 us (23%)
  other arithmetic  30.7 us (4%)
  between operations  21.2 us (2%)
  starting transfers between devices  17.1 us (2%)
  local copies, waits for them, and re-layouts  15.3 us (2%)
    all_gather x4, waiting for transfers between devices, per_device(): lax.all_gather(gram_old_half[cut], ('mp', 'heads'), axis=1, tiled=True)  327 us
    dot_general x22, matrix products, dot(): return jnp.dot(a, b, preferred_element_type=f32)  155 us
    reduce_scatter x1, waiting for transfers between devices, make_states(): mine = lax.psum_scatter(part, 'heads', scatter_dimension=1, tiled=True)  91.3 us
    ppermute x7, waiting for transfers between devices, shifted(): return lax.ppermute(block, axis, [(i, (i + shift) % n) for i in range(n)])  73.5 us
    all_gather x1, waiting for transfers between devices, make_states(): rows = lax.all_gather(half, 'heads', axis=1, tiled=True)  43.2 us
    dot_general x10, matrix products, token_inner(): lax.dot_general(left, right, (((0,), (0,)), ((), ())), preferred_element_...  41.2 us
  transfers between devices with their start and end apart: 21, of which 14 were waited for; matrix products, arithmetic and copies ran while one was open for 19% of the time, Pallas kernels for 0%

commit v1 on v0

--- a/solution.py
+++ b/solution.py
@@ -56,7 +56,14 @@
         away = lax.ppermute(pair, ("mp", "tok"), [(0, 1), (3, 2)])
         columns = jnp.where(k == t, pair, away)
         half = lax.dynamic_slice_in_dim(pair[0], k * (tokens // 2), tokens // 2, 0)
-        rows = lax.all_gather(half, "heads", axis=1, tiled=True)
+        ways, here = (lax.axis_size("heads"), lax.axis_index("heads"))
+        rows, reach = (half, 1)
+        while reach < ways:
+            theirs = lax.ppermute(rows, "heads", [(d, d ^ reach) for d in range(ways)])
+            mine_first = jnp.concatenate([rows, theirs], axis=1)
+            theirs_first = jnp.concatenate([theirs, rows], axis=1)
+            rows = jnp.where(here & reach == 0, mine_first, theirs_first)
+            reach = 2 * reach
         rows_other = lax.ppermute(rows, "mp", [(0, 1), (1, 0)])
         first = jnp.where(k == 0, rows, rows_other)
         second = jnp.where(k == 0, rows_other, rows)

time: 848 us -> 781 us (0.921)
  waiting for transfers between devices: 562 us -> 481 us
  starting transfers between devices: 17.1 us -> 25.6 us
    all_gather x4, waiting for transfers between devices: 327 us -> 81.7 us  [per_device(): lax.all_gather(gram_old_half[cut], ('mp', 'heads'), axis=1, tiled=True)]
    ppermute x0 -> x3, waiting for transfers between devices: none -> 141 us  [make_states(): theirs = lax.ppermute(rows, 'heads', [(d, d ^ reach) for d in range(ways)])]
    reduce_scatter x1, waiting for transfers between devices: 91.3 us -> 160 us  [make_states(): mine = lax.psum_scatter(part, 'heads', scatter_dimension=1, tiled=True)]
    all_gather x1 -> x0, waiting for transfers between devices: 43.2 us -> none  [make_states(): rows = lax.all_gather(half, 'heads', axis=1, tiled=True)]
  transfers between devices with their start and end apart: 21 -> 23, of which waited for: 14 -> 13; matrix products, arithmetic and copies ran while one was open for 19% -> 22% of each run, Pallas kernels for 0% -> 0%
where the time goes in v1:
time: 781 us; the launch traced here: 774 us
  waiting for transfers between devices  481 us (62%)
  matrix products  197 us (25%)
  other arithmetic  34.9 us (4%)
  starting transfers between devices  25.6 us (3%)
  between operations  23 us (3%)
  local copies, waits for them, and re-layouts  12.5 us (2%)
    reduce_scatter x1, waiting for transfers between devices, make_states(): mine = lax.psum_scatter(part, 'heads', scatter_dimension=1, tiled=True)  160 us
    dot_general x22, matrix products, dot(): return jnp.dot(a, b, preferred_element_type=f32)  156 us
    ppermute x3, waiting for transfers between devices, make_states(): theirs = lax.ppermute(rows, 'heads', [(d, d ^ reach) for d in range(ways)])  141 us
    all_gather x4, waiting for transfers between devices, per_device(): lax.all_gather(gram_old_half[cut], ('mp', 'heads'), axis=1, tiled=True)  81.7 us
    ppermute x7, waiting for transfers between devices, shifted(): return lax.ppermute(block, axis, [(i, (i + shift) % n) for i in range(n)])  72.2 us
    dot_general x10, matrix products, token_inner(): lax.dot_general(left, right, (((0,), (0,)), ((), ())), preferred_element_...  41.3 us
  transfers between devices with their start and end apart: 23, of which 13 were waited for; matrix products, arithmetic and copies ran while one was open for 22% of the time, Pallas kernels for 0%

profile of v1, /device:TPU:0, one launch (start us, length us, event | category | flops | bytes accessed | tf_op | source)
XLA Modules:
  0.0 774.5 jit_solution(13167531466207700208)
XLA Ops:
  9.2 9.4 %fusion.35 = bf16[512,4096]{1,0:T(8,128)(2,1)} fusion(bf16[1,1024,4096]{2,1,0:T(8,128)(2,1)} %param.7, bf16[1,512,1024]{2,1,0:T(8,128)(2,1)S(1)} %copy-done), kind=kOutput, calls=%fused_computation.49 | convolution fusion | flops 4297064448 | bytes 13631488 | tf_op jit(solution)/shard_map/dot_general | solution.py:13
  18.7 3.9 convert_element_type.56
  22.6 2.1 fusion.77
  26.7 160.2 %reduce-scatter.2.cloned.1.call-done = bf16[512,512]{1,0:T(8,128)(2,1)} async-done(((bf16[512,4096]{1,0:T(8,128)(2,1)}), bf16[512,512]{1,0:T(8,128)(2,1)}) %reduce-scatter.2.cloned.1.call-update) | async-done | bytes 524304 | tf_op jit(solution)/shard_map/reduce_scatter | solution.py:50
  186.9 1.3 fusion.53
  188.3 1.9 collective-permute-done
  190.3 1.5 collective-permute-start.1
  191.8 10.2 %collective-permute-done.1 = bf16[256,512]{1,0:T(8,128)(2,1)S(1)} collective-permute-done((bf16[256,512]{1,0:T(8,128)(2,1)S(1)}, bf16[256,512]{1,0:T(8,128)(2,1)S(1)}, u32[]{:S(2)}, u32[]{:S(2)}) %collective-permute-start.1) | collective-permute-done | bytes 262176 | tf_op jit(solution)/shard_map/ppermute | solution.py:62
  202.2 1.5 collective-permute-start.2
  203.8 29.6 %collective-permute-done.2 = bf16[256,1024]{1,0:T(8,128)(2,1)S(1)} collective-permute-done((bf16[256,1024]{1,0:T(8,128)(2,1)S(1)}, bf16[256,1024]{1,0:T(8,128)(2,1)S(1)}, u32[]{:S(2)}, u32[]{:S(2)}) %collective-permute-start.2) | collective-permute-done | bytes 524320 | tf_op jit(solution)/shard_map/ppermute | solution.py:62
  233.8 2.5 collective-permute-start.3
  236.3 101.2 %collective-permute-done.3 = bf16[256,2048]{1,0:T(8,128)(2,1)} collective-permute-done((bf16[256,2048]{1,0:T(8,128)(2,1)S(1)}, bf16[256,2048]{1,0:T(8,128)(2,1)}, u32[]{:S(2)}, u32[]{:S(2)}) %collective-permute-start.3) | collective-permute-done | bytes 1048608 | tf_op jit(solution)/shard_map/ppermute | solution.py:62
  337.4 3.0 maximum_select_fusion
  341.7 4.9 collective-permute-start.5
  346.6 5.9 convert_element_type.57
  352.5 10.7 %collective-permute-done.5 = bf16[2,512,512]{2,1,0:T(8,128)(2,1)} collective-permute-done((bf16[2,512,512]{2,1,0:T(8,128)(2,1)}, bf16[2,512,512]{2,1,0:T(8,128)(2,1)}, u32[]{:S(2)}, u32[]{:S(2)}) %collective-permute-start.5) | collective-permute-done | bytes 1048608 | tf_op jit(solution)/shard_map/ppermute | solution.py:56
  363.4 2.3 broadcast_select_fusion.1
  365.8 5.6 fusion.79
  371.4 3.9 collective-permute-start.7
  375.3 5.0 multiply_add_fusion.2
  380.3 4.9 multiply_add_fusion.1
  385.2 1.8 fusion.50
  387.1 72.2 %collective-permute-done.7 = bf16[512,512]{1,0:T(8,128)(2,1)S(1)} collective-permute-done((bf16[512,512]{1,0:T(8,128)(2,1)S(1)}, bf16[512,512]{1,0:T(8,128)(2,1)S(1)}, u32[]{:S(2)}, u32[]{:S(2)}) %collective-permute-start.7) | collective-permute-done | bytes 524320 | tf_op jit(solution)/shard_map/ppermute | solution.py:22
  459.5 8.6 %fusion.25 = f32[1024,512]{1,0:T(8,128)S(1)} fusion(bf16[4096,512]{1,0:T(8,128)(2,1)} %convert_element_type.57, bf16[1024,8192]{1,0:T(8,128)(2,1)} %all-gather.7.cloned.1.call-done, s32[]{:T(128)S(6)} %select_n.100), kind=kOutput, calls=%fused_computation.30 | convolution fusion | flops 4294967296 | bytes 14680068 | tf_op jit(solution)/shard_map/dot_general | solution.py:13
  469.4 6.5 fusion.21
  475.9 5.1 fusion.82
  481.0 2.3 collective-permute-start.9
  483.3 9.1 %fusion.13 = f32[1024,512]{1,0:T(8,128)S(1)} fusion(bf16[4096,512]{1,0:T(8,128)(2,1)} %collective-permute-done.6, bf16[1024,8192]{1,0:T(8,128)(2,1)} %all-gather.9.cloned.1.call-done, s32[]{:T(128)S(6)} %select_n.101), kind=kOutput, calls=%fused_computation.18 | convolution fusion | flops 4294967296 | bytes 14680068 | tf_op jit(solution)/shard_map/dot_general | solution.py:13
  493.5 6.6 fusion.17
  500.2 5.1 fusion.81
  505.4 8.5 %fusion.5 = f32[1024,512]{1,0:T(8,128)S(1)} fusion(bf16[4096,512]{1,0:T(8,128)(2,1)} %collective-permute-done.6, bf16[1024,8192]{1,0:T(8,128)(2,1)} %all-gather.11.cloned.1.call-done, s32[]{:T(128)S(6)} %select_n.101), kind=kOutput, calls=%fused_computation.10 | convolution fusion | flops 4294967296 | bytes 14680068 | tf_op jit(solution)/shard_map/dot_general | solution.py:13
  514.9 6.6 fusion.9
  521.5 5.3 fusion.80
  526.8 1.9 collective-permute-start.11
  528.8 2.9 fusion.85
  531.7 2.9 fusion.86
  534.6 3.0 fusion.87
  537.6 81.7 %all-gather.5.cloned.1.call-done = bf16[1024,8192]{1,0:T(8,128)(2,1)} async-done(((bf16[1024,512]{1,0:T(8,128)(2,1)}), bf16[1024,8192]{1,0:T(8,128)(2,1)}) %all-gather.5.cloned.1.call-update) | async-done | bytes 16777232 | tf_op jit(solution)/shard_map/all_gather | solution.py:89
  619.3 8.3 %fusion.29 = f32[1024,512]{1,0:T(8,128)S(1)} fusion(bf16[4096,512]{1,0:T(8,128)(2,1)} %collective-permute-done.6, bf16[1024,8192]{1,0:T(8,128)(2,1)} %all-gather.5.cloned.1.call-done, s32[]{:T(128)S(6)} %select_n.101), kind=kOutput, calls=%fused_computation.34 | convolution fusion | flops 4294967296 | bytes 14680068 | tf_op jit(solution)/shard_map/dot_general | solution.py:13
  628.7 6.7 fusion.33
  635.4 3.5 fusion.83
  639.0 1.5 collective-permute-start.8
  641.9 9.2 %fusion.31 = f32[1024,512]{1,0:T(8,128)S(1)} fusion(bf16[1024,8192]{1,0:T(8,128)(2,1)} %all-gather.5.cloned.1.call-done, s32[]{:T(128)S(6)} %select_n.100, bf16[1024,512]{1,0:T(8,128)(2,1)} %get-tuple-element.29, bf16[1024,512]{1,0:T(8,128)(2,1)} %get-tuple-element.31, bf16[1024,512]{1,0:T(8,128)(2,1)} %get-tuple-element.33, ...), kind=kOutput, calls=%fused_computation.36 | convolution fusion | flops 4311744512 | bytes 14680068 | tf_op jit(solution)/shard_map/dot_general | solution.py:13
  651.1 8.8 %fusion.23 = f32[1024,512]{1,0:T(8,128)S(1)} fusion(bf16[1024,8192]{1,0:T(8,128)(2,1)} %all-gather.7.cloned.1.call-done, s32[]{:T(128)S(6)} %select_n.100, bf16[1024,512]{1,0:T(8,128)(2,1)} %get-tuple-element.29, bf16[1024,512]{1,0:T(8,128)(2,1)} %get-tuple-element.31, bf16[1024,512]{1,0:T(8,128)(2,1)} %get-tuple-element.33, ...), kind=kOutput, calls=%fused_computation.28 | convolution fusion | flops 4311744512 | bytes 14680068 | tf_op jit(solution)/shard_map/dot_general | solution.py:13
  660.0 10.0 %fusion.15 = f32[1024,512]{1,0:T(8,128)} fusion(bf16[1024,8192]{1,0:T(8,128)(2,1)} %all-gather.9.cloned.1.call-done, s32[]{:T(128)S(6)} %select_n.100, bf16[1024,512]{1,0:T(8,128)(2,1)} %get-tuple-element.29, bf16[1024,512]{1,0:T(8,128)(2,1)} %get-tuple-element.31, bf16[1024,512]{1,0:T(8,128)(2,1)} %get-tuple-element.33, ...), kind=kOutput, calls=%fused_computation.20 | convolution fusion | flops 4311744512 | bytes 14680068 | tf_op jit(solution)/shard_map/dot_general | solution.py:13
  670.0 10.1 %fusion.7 = f32[1024,512]{1,0:T(8,128)} fusion(bf16[1024,8192]{1,0:T(8,128)(2,1)} %all-gather.11.cloned.1.call-done, s32[]{:T(128)S(6)} %select_n.100, bf16[1024,512]{1,0:T(8,128)(2,1)} %get-tuple-element.29, bf16[1024,512]{1,0:T(8,128)(2,1)} %get-tuple-element.31, bf16[1024,512]{1,0:T(8,128)(2,1)} %get-tuple-element.33, ...), kind=kOutput, calls=%fused_computation.12 | convolution fusion | flops 4311744512 | bytes 14680068 | tf_op jit(solution)/shard_map/dot_general | solution.py:13
  681.6 1.3 constant_dynamic-update-slice_fusion.1
  682.9 1.3 constant_dynamic-update-slice_fusion
  684.2 8.6 %fusion.27 = f32[1024,512]{1,0:T(8,128)S(1)} fusion(bf16[4096,512]{1,0:T(8,128)(2,1)S(1)} %constant_dynamic-update-slice_fusion, bf16[1024,8192]{1,0:T(8,128)(2,1)} %all-gather.5.cloned.1.call-done, s32[]{:T(128)S(6)} %select_n.101), kind=kOutput, calls=%fused_computation.32 | convolution fusion | flops 4294967296 | bytes 14680068 | tf_op jit(solution)/shard_map/dot_general | solution.py:13
  692.9 3.1 multiply_reduce_fusion.7
  696.0 7.1 fusion.19
  703.1 3.2 multiply_reduce_fusion.6
  707.6 8.3 %fusion.11 = f32[1024,512]{1,0:T(8,128)S(1)} fusion(bf16[4096,512]{1,0:T(8,128)(2,1)} %copy-done.24, bf16[1024,8192]{1,0:T(8,128)(2,1)} %all-gather.9.cloned.1.call-done, s32[]{:T(128)S(6)} %select_n.101), kind=kOutput, calls=%fused_computation.16 | convolution fusion | flops 4294967296 | bytes 14680068 | tf_op jit(solution)/shard_map/dot_general | solution.py:13
  715.9 3.1 multiply_reduce_fusion.5
  719.6 8.3 %fusion.3 = f32[1024,512]{1,0:T(8,128)S(1)} fusion(bf16[4096,512]{1,0:T(8,128)(2,1)} %copy-done.24, bf16[1024,8192]{1,0:T(8,128)(2,1)} %all-gather.11.cloned.1.call-done, s32[]{:T(128)S(6)} %select_n.101), kind=kOutput, calls=%fused_computation.8 | convolution fusion | flops 4294967296 | bytes 14680068 | tf_op jit(solution)/shard_map/dot_general | solution.py:13
  728.0 3.1 multiply_reduce_fusion.4
  735.5 1.5 collective-permute-start.14
  736.9 2.1 collective-permute-done.14
  739.1 1.4 collective-permute-start.15
  740.5 2.1 collective-permute-done.15
  742.6 3.5 collective-permute-done.16
  746.2 1.5 collective-permute-start.17
  747.7 2.9 collective-permute-done.17
  752.6 14.1 %fusion = (f32[4096,512]{1,0:T(8,128)}, f32[4096,512]{1,0:T(8,128)}) fusion(f32[1024,512]{1,0:T(8,128)} %get-tuple-element.42, f32[1024,512]{1,0:T(8,128)} %get-tuple-element.41, f32[1024,512]{1,0:T(8,128)} %get-tuple-element.40, f32[1024,512]{1,0:T(8,128)} %get-tuple-element.39, f32[1024,512]{1,0:T(8,128)} %get-tuple-element.30, ...), kind=kLoop, calls=%fused_computation.2 | loop fusion | flops 20971520 | bytes 41943044 | tf_op jit(solution)/shard_map/sub | solution.py:133
  (114 shorter events, 15.1 us)
Async XLA Ops:
  8.0 1.2 copy-start
  8.0 178.9 %reduce-scatter.2.cloned.1.call-start = ((), (), s32[]{:S(2)}) async-start(), calls=%async_computation.1 | async-start | bytes 4718592 | tf_op jit(solution)/shard_map/reduce_scatter | solution.py:50
  18.6 440.8 %all-gather.7.cloned.1.call-start = ((), (), s32[]{:S(2)}) async-start(), calls=%async_computation.3 | async-start | bytes 17825792 | tf_op jit(solution)/shard_map/all_gather | solution.py:89
  24.8 458.5 %all-gather.9.cloned.1.call-start = ((), (), s32[]{:S(2)}) async-start(), calls=%async_computation.4 | async-start | bytes 17825792 | tf_op jit(solution)/shard_map/all_gather | solution.py:89
  25.4 480.0 %all-gather.11.cloned.1.call-start = ((), (), s32[]{:S(2)}) async-start(), calls=%async_computation.5 | async-start | bytes 17825792 | tf_op jit(solution)/shard_map/all_gather | solution.py:89
  25.9 593.4 %all-gather.5.cloned.1.call-start = ((), (), s32[]{:S(2)}) async-start(), calls=%async_computation.2 | async-start | bytes 17825792 | tf_op jit(solution)/shard_map/all_gather | solution.py:89
  188.2 2.0 collective-permute-start
  190.3 11.8 %collective-permute-start.1 = (bf16[256,512]{1,0:T(8,128)(2,1)S(1)}, bf16[256,512]{1,0:T(8,128)(2,1)S(1)}, u32[]{:S(2)}, u32[]{:S(2)}) collective-permute-start(bf16[256,512]{1,0:T(8,128)(2,1)S(1)} %constant_dynamic-slice_fusion), channel_id=1, source_target_pairs={{0,2},{2,0},{4,6},{6,4},{8,10},{10,8},{12,14},{14,12},{1,3},{3,1},... | collective-permute-start | bytes 786440 | tf_op jit(solution)/shard_map/ppermute | solution.py:62
  202.2 31.2 %collective-permute-start.2 = (bf16[256,1024]{1,0:T(8,128)(2,1)S(1)}, bf16[256,1024]{1,0:T(8,128)(2,1)S(1)}, u32[]{:S(2)}, u32[]{:S(2)}) collective-permute-start(bf16[256,1024]{1,0:T(8,128)(2,1)S(1)} %maximum_select_fusion.2), channel_id=1, source_target_pairs={{0,4},{2,6},{4,0},{6,2},{8,12},{10,14},{12,8},{14,10},{1,5},{3,7},... | collective-permute-start | bytes 1572872 | tf_op jit(solution)/shard_map/ppermute | solution.py:62
  233.7 2.5 copy-start.18
  233.8 103.7 %collective-permute-start.3 = (bf16[256,2048]{1,0:T(8,128)(2,1)S(1)}, bf16[256,2048]{1,0:T(8,128)(2,1)}, u32[]{:S(2)}, u32[]{:S(2)}) collective-permute-start(bf16[256,2048]{1,0:T(8,128)(2,1)S(1)} %maximum_select_fusion.1), channel_id=1, source_target_pairs={{0,8},{2,10},{4,12},{6,14},{8,0},{10,2},{12,4},{14,6},{1,9},{3,11}... | collective-permute-start | bytes 3145736 | tf_op jit(solution)/shard_map/ppermute | solution.py:62
  340.4 12.1 %copy-start.16 = (bf16[256,4096]{1,0:T(8,128)(2,1)}, bf16[256,4096]{1,0:T(8,128)(2,1)S(1)}, u32[]{:S(2)}) copy-start(bf16[256,4096]{1,0:T(8,128)(2,1)S(1)} %maximum_select_fusion) | copy-start | bytes 6291460
  340.4 23.0 %collective-permute-start.4 = (bf16[256,4096]{1,0:T(8,128)(2,1)S(1)}, bf16[256,4096]{1,0:T(8,128)(2,1)}, u32[]{:S(2)}, u32[]{:S(2)}) collective-permute-start(bf16[256,4096]{1,0:T(8,128)(2,1)S(1)} %maximum_select_fusion), channel_id=1, source_target_pairs={{0,16},{16,0},{1,17},{17,1},{2,18},{18,2},{3,19},{19,3},{4,20},{20... | collective-permute-start | bytes 6291464 | tf_op jit(solution)/shard_map/ppermute | solution.py:67
  341.7 21.5 %collective-permute-start.5 = (bf16[2,512,512]{2,1,0:T(8,128)(2,1)}, bf16[2,512,512]{2,1,0:T(8,128)(2,1)}, u32[]{:S(2)}, u32[]{:S(2)}) collective-permute-start(bf16[2,512,512]{2,1,0:T(8,128)(2,1)} %pad_maximum_fusion.6), channel_id=1, source_target_pairs={{0,1},{17,16},{2,3},{19,18},{4,5},{21,20},{6,7},{23,22},{8,9},{25,... | collective-permute-start | bytes 3145736 | tf_op jit(solution)/shard_map/ppermute | solution.py:56
  352.5 115.6 %collective-permute-start.6 = (bf16[4096,512]{1,0:T(8,128)(2,1)}, bf16[4096,512]{1,0:T(8,128)(2,1)}, u32[]{:S(2)}, u32[]{:S(2)}) collective-permute-start(bf16[4096,512]{1,0:T(8,128)(2,1)} %convert_element_type.57), channel_id=1, source_target_pairs={{0,1},{1,0},{2,3},{3,2},{4,5},{5,4},{6,7},{7,6},{8,9},{9,8},{10,11... | collective-permute-start | bytes 12582920 | tf_op jit(solution)/shard_map/ppermute | solution.py:22
  352.5 10.9 %copy-start.17 = (bf16[256,4096]{1,0:T(8,128)(2,1)S(1)}, bf16[256,4096]{1,0:T(8,128)(2,1)}, u32[]{:S(2)}) copy-start(bf16[256,4096]{1,0:T(8,128)(2,1)} %copy-done.16) | copy-start | bytes 6291460
  363.4 11.9 %slice-start = ((s8[8388608]{0:T(1024)(128)(4,1)}), s8[4194304]{0:T(1024)(128)(4,1)S(1)}, s32[]{:S(2)}) async-start(s8[8388608]{0:T(1024)(128)(4,1)} %bitcast.57), calls=%async_computation.6 | async-start | bytes 8388608
  365.7 19.5 %copy-start.2 = (bf16[256,4096]{1,0:T(8,128)(2,1)}, bf16[256,4096]{1,0:T(8,128)(2,1)S(1)}, u32[]{:S(2)}) copy-start(bf16[256,4096]{1,0:T(8,128)(2,1)S(1)} %get-tuple-element.22) | copy-start | bytes 6291460
  365.7 9.6 %slice-start.1 = ((s8[8388608]{0:T(1024)(128)(4,1)}), s8[4194304]{0:T(1024)(128)(4,1)S(1)}, s32[]{:S(2)}) async-start(s8[8388608]{0:T(1024)(128)(4,1)} %bitcast.57), calls=%async_computation.7 | async-start | bytes 8388608
  371.4 9.0 %slice-start.2 = ((s8[8388608]{0:T(1024)(128)(4,1)}), s8[4194304]{0:T(1024)(128)(4,1)S(1)}, s32[]{:S(2)}) async-start(s8[8388608]{0:T(1024)(128)(4,1)} %bitcast.61), calls=%async_computation.8 | async-start | bytes 8388608
  371.4 9.0 %slice-start.3 = ((s8[8388608]{0:T(1024)(128)(4,1)}), s8[4194304]{0:T(1024)(128)(4,1)S(1)}, s32[]{:S(2)}) async-start(s8[8388608]{0:T(1024)(128)(4,1)} %bitcast.61), calls=%async_computation.9 | async-start | bytes 8388608
  371.4 87.8 %collective-permute-start.7 = (bf16[512,512]{1,0:T(8,128)(2,1)S(1)}, bf16[512,512]{1,0:T(8,128)(2,1)S(1)}, u32[]{:S(2)}, u32[]{:S(2)}) collective-permute-start(bf16[512,512]{1,0:T(8,128)(2,1)S(1)} %get-tuple-element.27), channel_id=1, source_target_pairs={{0,1},{1,0},{2,3},{3,2},{4,5},{5,4},{6,7},{7,6},{8,9},{9,8},{10,11... | collective-permute-start | bytes 1572872 | tf_op jit(solution)/shard_map/ppermute | solution.py:22
  459.5 9.9 %copy-start.27 = (bf16[1024,8192]{1,0:T(8,128)(2,1)S(1)}, bf16[1024,8192]{1,0:T(8,128)(2,1)}, u32[]{:S(2)}) copy-start(bf16[1024,8192]{1,0:T(8,128)(2,1)} %all-gather.7.cloned.1.call-done) | copy-start | bytes 50331652
  468.1 7.8 %copy-start.13 = (bf16[512,1024]{1,0:T(8,128)(2,1)S(1)}, bf16[512,1024]{1,0:T(8,128)(2,1)}, u32[]{:S(2)}) copy-start(bf16[512,1024]{1,0:T(8,128)(2,1)} %get-tuple-element.18) | copy-start | bytes 3145732
  481.0 199.4 %collective-permute-start.9 = (bf16[1024,512]{1,0:T(8,128)(2,1)}, bf16[1024,512]{1,0:T(8,128)(2,1)}, u32[]{:S(2)}, u32[]{:S(2)}) collective-permute-start(bf16[1024,512]{1,0:T(8,128)(2,1)} %get-tuple-element.33), channel_id=1, source_target_pairs={{0,1},{1,0},{2,3},{3,2},{4,5},{5,4},{6,7},{7,6},{8,9},{9,8},{10,11... | collective-permute-start | bytes 3145736 | tf_op jit(solution)/shard_map/ppermute | solution.py:22
  483.3 10.3 %copy-start.26 = (bf16[1024,8192]{1,0:T(8,128)(2,1)S(1)}, bf16[1024,8192]{1,0:T(8,128)(2,1)}, u32[]{:S(2)}) copy-start(bf16[1024,8192]{1,0:T(8,128)(2,1)} %all-gather.9.cloned.1.call-done) | copy-start | bytes 50331652
  493.5 6.6 copy-start.10
  505.3 176.4 %collective-permute-start.10 = (bf16[1024,512]{1,0:T(8,128)(2,1)}, bf16[1024,512]{1,0:T(8,128)(2,1)}, u32[]{:S(2)}, u32[]{:S(2)}) collective-permute-start(bf16[1024,512]{1,0:T(8,128)(2,1)} %get-tuple-element.31), channel_id=1, source_target_pairs={{0,1},{1,0},{2,3},{3,2},{4,5},{5,4},{6,7},{7,6},{8,9},{9,8},{10,11... | collective-permute-start | bytes 3145736 | tf_op jit(solution)/shard_map/ppermute | solution.py:22
  505.4 9.5 %copy-start.25 = (bf16[1024,8192]{1,0:T(8,128)(2,1)S(1)}, bf16[1024,8192]{1,0:T(8,128)(2,1)}, u32[]{:S(2)}) copy-start(bf16[1024,8192]{1,0:T(8,128)(2,1)} %all-gather.11.cloned.1.call-done) | copy-start | bytes 50331652
  514.9 6.6 copy-start.8
  521.5 7.3 copy-start.14
  521.5 10.2 %copy-start.11 = (bf16[512,1024]{1,0:T(8,128)(2,1)S(1)}, bf16[512,1024]{1,0:T(8,128)(2,1)}, u32[]{:S(2)}) copy-start(bf16[512,1024]{1,0:T(8,128)(2,1)} %get-tuple-element.19) | copy-start | bytes 3145732
  526.8 156.1 %collective-permute-start.11 = (bf16[1024,512]{1,0:T(8,128)(2,1)}, bf16[1024,512]{1,0:T(8,128)(2,1)}, u32[]{:S(2)}, u32[]{:S(2)}) collective-permute-start(bf16[1024,512]{1,0:T(8,128)(2,1)} %get-tuple-element.29), channel_id=1, source_target_pairs={{0,1},{1,0},{2,3},{3,2},{4,5},{5,4},{6,7},{7,6},{8,9},{9,8},{10,11... | collective-permute-start | bytes 3145736 | tf_op jit(solution)/shard_map/ppermute | solution.py:22
  619.3 9.4 %copy-start.28 = (bf16[1024,8192]{1,0:T(8,128)(2,1)S(1)}, bf16[1024,8192]{1,0:T(8,128)(2,1)}, u32[]{:S(2)}) copy-start(bf16[1024,8192]{1,0:T(8,128)(2,1)} %all-gather.5.cloned.1.call-done) | copy-start | bytes 50331652
  628.7 6.7 copy-start.3
  635.4 5.1 copy-start.21
  635.4 5.1 copy-start.22
  635.4 5.1 copy-start.23
  639.0 53.9 %copy-start.7 = (f32[1024,512]{1,0:T(8,128)}, f32[1024,512]{1,0:T(8,128)S(1)}, u32[]{:S(2)}) copy-start(f32[1024,512]{1,0:T(8,128)S(1)} %get-tuple-element.36) | copy-start | bytes 6291460
  639.0 41.3 %collective-permute-start.8 = (bf16[1024,512]{1,0:T(8,128)(2,1)S(1)}, bf16[1024,512]{1,0:T(8,128)(2,1)S(1)}, u32[]{:S(2)}, u32[]{:S(2)}) collective-permute-start(bf16[1024,512]{1,0:T(8,128)(2,1)S(1)} %get-tuple-element.35), channel_id=1, source_target_pairs={{0,1},{1,0},{2,3},{3,2},{4,5},{5,4},{6,7},{7,6},{8,9},{9,8},{10,11... | collective-permute-start | bytes 3145736 | tf_op jit(solution)/shard_map/ppermute | solution.py:22
  641.2 38.8 %collective-permute-start.12 = (bf16[512,512]{1,0:T(8,128)(2,1)S(1)}, bf16[512,512]{1,0:T(8,128)(2,1)S(1)}, u32[]{:S(2)}, u32[]{:S(2)}) collective-permute-start(bf16[512,512]{1,0:T(8,128)(2,1)S(1)} %get-tuple-element.37), channel_id=1, source_target_pairs={{0,1},{1,0},{2,3},{3,2},{4,5},{5,4},{6,7},{7,6},{8,9},{9,8},{10,11... | collective-permute-start | bytes 1572872 | tf_op jit(solution)/shard_map/ppermute | solution.py:22
  684.2 11.7 %copy-start.24 = (bf16[4096,512]{1,0:T(8,128)(2,1)}, bf16[4096,512]{1,0:T(8,128)(2,1)S(1)}, u32[]{:S(2)}) copy-start(bf16[4096,512]{1,0:T(8,128)(2,1)S(1)} %constant_dynamic-update-slice_fusion) | copy-start | bytes 12582916
  696.0 7.1 copy-start.4
  696.0 7.1 copy-start.15
  707.5 8.3 %copy-start.5 = (f32[1024,512]{1,0:T(8,128)S(1)}, f32[1024,512]{1,0:T(8,128)}, u32[]{:S(2)}) copy-start(f32[1024,512]{1,0:T(8,128)} %get-tuple-element.32) | copy-start | bytes 6291460
  707.5 8.3 %copy-start.12 = (bf16[512,1024]{1,0:T(8,128)(2,1)S(1)}, bf16[512,1024]{1,0:T(8,128)(2,1)}, u32[]{:S(2)}) copy-start(bf16[512,1024]{1,0:T(8,128)(2,1)} %get-tuple-element.19) | copy-start | bytes 3145732
  707.5 8.3 %copy-start.20 = (f32[1024,512]{1,0:T(8,128)S(1)}, f32[1024,512]{1,0:T(8,128)}, u32[]{:S(2)}) copy-start(f32[1024,512]{1,0:T(8,128)} %fusion.15) | copy-start | bytes 6291460
  719.6 8.3 %copy-start.6 = (f32[1024,512]{1,0:T(8,128)S(1)}, f32[1024,512]{1,0:T(8,128)}, u32[]{:S(2)}) copy-start(f32[1024,512]{1,0:T(8,128)} %get-tuple-element.30) | copy-start | bytes 6291460
  719.6 8.3 %copy-start.9 = (bf16[512,1024]{1,0:T(8,128)(2,1)S(1)}, bf16[512,1024]{1,0:T(8,128)(2,1)}, u32[]{:S(2)}) copy-start(bf16[512,1024]{1,0:T(8,128)(2,1)} %get-tuple-element.20) | copy-start | bytes 3145732
  719.6 8.3 %copy-start.19 = (f32[1024,512]{1,0:T(8,128)S(1)}, f32[1024,512]{1,0:T(8,128)}, u32[]{:S(2)}) copy-start(f32[1024,512]{1,0:T(8,128)} %fusion.7) | copy-start | bytes 6291460
  734.3 1.1 collective-permute-start.13
  735.5 3.5 collective-permute-start.14
  739.1 3.5 collective-permute-start.15
  742.6 3.5 collective-permute-start.16
  746.2 4.4 collective-permute-start.17
  752.6 14.1 %copy-start.1 = (bf16[1,512,1024]{2,1,0:T(8,128)(2,1)S(1)}, bf16[1,512,1024]{2,1,0:T(8,128)(2,1)}, u32[]{:S(2)}) copy-start(bf16[1,512,1024]{2,1,0:T(8,128)(2,1)} %param.6) | copy-start | bytes 3145732
Sparse Core Ops, SparseCore 0:
  18.8 168.0 reduce-scatter.1
Sparse Core Ops, SparseCore 1:
  24.8 147.6 all-gather.6
  174.7 179.9 all-gather.8
  356.8 132.0 all-gather.10
  491.1 128.1 all-gather.4
